TPU v7x, 32 devices: a whole 2x2x4 slice. The times are simulated.
32 devices in a mesh: groups: 2 (over y), pts: 4 (over z), blk: 2 (over x), rep: 2 (over core).
Axes of the slice: x: 2, y: 2, z: 4, core: 2. Of those that a mesh axis runs over, the one named last changes fastest.
Arguments:
- points_x: bfloat16 [32768, 512], P(('groups', 'pts', 'blk')), parts along dimension 0, may hold values from -6 to 6
- coords: float32 [3, 32768], P(None, ('groups', 'pts', 'blk')), parts along dimension 1, may hold values from 0 to 32
- panels: bfloat16 [32768, 256], P(('groups', 'pts', 'blk')), parts along dimension 0, may hold values from -0.09375 to 0.09375
- coupling: bfloat16 [2048, 256], P(('groups', 'pts')), parts along dimension 0, may hold values from -0.375 to 0.375
- near_list: int32 [64, 4], P(('groups', 'pts', 'blk')), parts along dimension 0, may hold values from -1 to 31, as said below
- order: int32 [32768], P(('groups', 'pts', 'blk')), parts along dimension 0, may hold values from 0 to 16383, as said below
Outputs:
- product: float32 [32768, 512], P(('groups', 'pts', 'blk', 'rep')), parts along dimension 0
There are 2 independent parts, one for each index of `groups`. A program takes and returns all parts, laid end to end along the dimension named above; each array names one. Nothing has to cross between parts.
Inputs may be any that keep to these rules, and one draw needn't show every extreme that they name: `near_list`: each near-field entry is -1 or a leaf among the same 4 consecutive leaves (aligned) as its own leaf; slot 0 is the leaf itself; live entries of a row are distinct and come before empty ones; some leaf of every draw has all 4 slots live. `order`: each aligned block of 2048 tree positions holds a permutation of the same block of point indices.
All inputs are finite; a program needn't handle non-finite values.
Results may differ from a plain program's by a relative error of at most 0.00036.
Values sent between devices are 32-bit elements; how exact they have to be, the bound alone decides.
A program may use at most 64 MiB of HBM per device.

v0:
```python
import jax
import jax.numpy as jnp
from jax import lax
from jax.sharding import PartitionSpec as P

LEAF = 512
NEAR = 4


spread = 1.0 / (2.0 * 0.1 * 0.1)


def partner_2(value, axis, stride):
    mask = 2**stride
    pairs = [(source, source ^ mask) for source in range(lax.axis_size(axis))]
    return lax.ppermute(value, axis, pairs)


def kernel_block(left, right):
    gap = left[:, :, None] - right[:, None, :]
    dist = jnp.sum(gap * gap, axis=0)
    return jnp.exp(-dist * spread).astype(jnp.bfloat16)


def on_device(points_x, coords, panels, coupling, near_list, order):
    rows = points_x.shape[0]
    nrhs = points_x.shape[1]
    leaf_count = rows // LEAF
    blk_count = lax.axis_size("blk")
    rep_count = lax.axis_size("rep")
    rep_index = lax.axis_index("rep")
    seg_index = lax.axis_index("pts")
    start = (seg_index * blk_count + lax.axis_index("blk")) * rows
    base_leaf = start // LEAF
    local = order - start
    tree_x = jnp.take(points_x, local, axis=0)
    tree_c = jnp.take(coords, local, axis=1)
    leaves_x = tree_x.reshape(leaf_count, LEAF, nrhs)
    leaves_c = tree_c.reshape(3, leaf_count, LEAF)

    def leaf_sum(leaf, slot_list):
        left = lax.dynamic_index_in_dim(leaves_c, leaf, 1, keepdims=False)
        total = jnp.zeros((LEAF, nrhs), jnp.float32)
        for slot in slot_list:
            ident = near_list[leaf, slot]
            other = jnp.maximum(ident - base_leaf, 0)

            def add_block(acc):
                right = lax.dynamic_index_in_dim(leaves_c, other, 1, keepdims=False)
                values = lax.dynamic_index_in_dim(leaves_x, other, 0, keepdims=False)
                return acc + jnp.dot(
                    kernel_block(left, right), values, preferred_element_type=jnp.float32
                )

            total = lax.cond(ident >= 0, add_block, lambda acc: acc, total)
        return total

    def near_rows(leaf):
        return leaf_sum(leaf, [rep_index + turn * rep_count for turn in range(NEAR // rep_count)])

    near_part = lax.map(near_rows, jnp.arange(leaf_count, dtype=jnp.int32)).reshape(rows, nrhs)
    near_own = lax.psum_scatter(near_part, "rep", scatter_dimension=0, tiled=True)
    part_coef = lax.dot_general(
        panels, tree_x, (((0,), (0,)), ((), ())), preferred_element_type=jnp.float32
    )
    coef = lax.psum(part_coef, "blk")
    level_count = min(lax.axis_size("pts").bit_length() - 1, 4)
    running = coef
    incoming = jnp.zeros_like(coef)
    for bit in range(level_count):
        partner = partner_2(running, "pts", bit)
        incoming = incoming + 2.0 ** (-0.5 * bit) * partner
        running = running + partner
    mixed = jnp.dot(coupling.astype(jnp.float32), incoming, precision=lax.Precision.HIGHEST).astype(
        jnp.bfloat16
    )
    half = rows // rep_count
    own_panels = lax.dynamic_slice_in_dim(panels, rep_index * half, half, 0)
    far = jnp.dot(own_panels, mixed, preferred_element_type=jnp.float32)
    return near_own * LEAF ** (-0.5) + far


def solution(mesh):
    placed = (
        P(("groups", "pts", "blk"), None),
        P(None, ("groups", "pts", "blk")),
        P(("groups", "pts", "blk"), None),
        P(("groups", "pts"), None),
        P(("groups", "pts", "blk"), None),
        P(("groups", "pts", "blk")),
    )
    return jax.shard_map(
        on_device,
        mesh=mesh,
        in_specs=placed,
        out_specs=P(("groups", "pts", "blk", "rep"), None),
        check_vma=False,
    )
```

profile of v0, /device:TPU:31, one launch (start us, length us, event | category | flops | bytes accessed | tf_op | source)
XLA Modules:
  0.0 130.0 jit_solution(8597873059099104402)
XLA Ops:
  7.4 0.9 compare_and_fusion
  8.2 0.7 fusion.23
  9.0 9.2 %gather_fusion.1 = bf16[2048,512]{1,0:T(8,128)(2,1)} fusion(bf16[2048,512]{1,0:T(8,128)(2,1)S(1)} %copy-done, s32[2048]{0:T(1024)S(1)} %fusion.23), kind=kCustom, calls=%fused_computation.1 | custom fusion | bytes 4202496 | tf_op jit(solution)/shard_map/jit(_take)/gather | solution.py:36
  18.2 3.5 %fusion.15 = f32[256,512]{0,1:T(8,128)} fusion(bf16[2048,256]{1,0:T(8,128)(2,1)S(1)} %copy-done.1, bf16[2048,512]{1,0:T(8,128)(2,1)} %gather_fusion.1, pred[2048]{0:T(1024)(128)(4,1)S(1)} %compare_and_fusion), kind=kOutput, calls=%fused_computation.28 | convolution fusion | flops 537919488 | bytes 3672064 | tf_op jit(solution)/shard_map/dot_general | solution.py:63
  22.2 7.6 %gather_fusion = f32[2048,3]{1,0:T(8,128)} fusion(f32[3,2048]{0,1:T(8,128)S(1)} %copy.9, s32[2048]{0:T(1024)S(1)} %fusion.23), kind=kCustom, calls=%fused_computation | custom fusion | bytes 57344 | tf_op jit(solution)/shard_map/jit(_take)/gather | solution.py:37
  29.8 1.6 %copy.10 = f32[3,4,512]{2,0,1:T(4,128)S(1)} copy(f32[3,4,512]{0,2,1:T(8,128)} %bitcast.39) | data formatting | bytes 49152 | tf_op jit(solution)/shard_map/jit(_take)/gather | solution.py:37
  31.4 2.8 %broadcast_select_fusion = bf16[4,512,512]{2,1,0:T(8,128)(2,1)} fusion(bf16[4,512,512]{2,1,0:T(8,128)(2,1)} %bitcast.37, pred[4,512]{1,0:T(4,128)(4,1)S(1)} %broadcast_in_dim.47), kind=kLoop, calls=%fused_computation.27 | loop fusion | flops 1048576 | bytes 4196352 | tf_op jit(solution)/shard_map/jit(_take)/select_n | solution.py:36
  34.1 43.1 %while.12 = (s32[]{:T(128)}, f32[4,512,512]{2,1,0:T(8,128)}, s32[4]{0:T(128)S(1)}, s32[4,4]{1,0:T(4,128)S(1)}, s32[]{:T(128)}, /*index=5*/s32[]{:T(128)}, s32[]{...) while((s32[]{:T(128)}, f32[4,512,512]{2,1,0:T(8,128)}, ...), condition=%wide.region_7.8_spmd, body=%wide.region_0.7_spmd.sunk | while | flops 542900224 | bytes 10547645 | solution.py:61
  34.1 0.6 dynamic_slice.61
  36.8 0.7 fusion.32
  38.7 2.5 %conditional.4 = (f32[512,512]{1,0:T(8,128)S(1)}) conditional(s32[]{:T(128)} %convert_element_type.30, () %tuple.55, (f32[3,512]{1,0:T(4,128)S(1)}, s32[]{:T(128)}, f32[3,4,512]{2,0,1:T(4,128)S(1)}, bf16[4,512,512]{2,1,0:T(8,128)(2,1)}, s32[]{:T(128)}, /*index=5*/s32[]{:T(128)}) %tuple.56), branch_computations={%region_1.1_spmd, %region_2.3_spmd} | conditional | flops 271319040 | bytes 3694666 | solution.py:55
  39.4 0.4 multiply_reduce_fusion
  39.7 1.5 %fusion = f32[512,512]{1,0:T(8,128)S(1)} fusion(f32[512,512]{1,0:T(8,128)S(1)} %multiply_reduce_fusion, bf16[4,512,512]{2,1,0:T(8,128)(2,1)} %get-tuple-element.142, s32[]{:T(128)S(6)} %select_n.43), kind=kOutput, calls=%fused_computation.4 | convolution fusion | flops 269221888 | bytes 2621444 | tf_op jit(solution)/shard_map/while/body/eval_jaxpr/cond/branch_1_fun/dot_general | solution.py:51
  41.2 2.6 %conditional.5 = (f32[1,512,512]{2,1,0:T(8,128)S(1)}) conditional(s32[]{:T(128)} %convert_element_type.29, f32[512,512]{1,0:T(8,128)S(1)} %get-tuple-element.291, (f32[3,512]{1,0:T(4,128)S(1)}, s32[]{:T(128)}, s32[]{:T(128)}, f32[3,4,512]{2,0,1:T(4,128)S(1)}, bf16[4,512,512]{2,1,0:T(8,128)(2,1)}, /*index=5*/f32[512,512]{1,0:T(8,128)S(1)}) %tuple.63), branch_computations={%region_4.4_spmd, %region_5.6_spmd} | conditional | flops 271581184 | bytes 4743208 | solution.py:55
  41.9 0.4 multiply_reduce_fusion.1
  42.3 1.5 %fusion.6 = f32[1,512,512]{2,1,0:T(8,128)S(1)} fusion(f32[512,512]{1,0:T(8,128)S(1)} %get-tuple-element.143, f32[512,512]{1,0:T(8,128)S(1)} %multiply_reduce_fusion.1, bf16[4,512,512]{2,1,0:T(8,128)(2,1)} %get-tuple-element.148, s32[]{:T(128)S(6)} %max.8), kind=kOutput, calls=%fused_computation.13 | convolution fusion | flops 269484032 | bytes 3670020 | tf_op jit(solution)/shard_map/while/body/eval_jaxpr/cond/branch_1_fun/dot_general | solution.py:51
  43.8 1.0 constant_dynamic-update-slice_fusion.2
  44.9 0.6 dynamic_slice.61
  47.5 0.7 fusion.32
  49.5 2.5 %conditional.4 = (f32[512,512]{1,0:T(8,128)S(1)}) conditional(s32[]{:T(128)} %convert_element_type.30, () %tuple.55, (f32[3,512]{1,0:T(4,128)S(1)}, s32[]{:T(128)}, f32[3,4,512]{2,0,1:T(4,128)S(1)}, bf16[4,512,512]{2,1,0:T(8,128)(2,1)}, s32[]{:T(128)}, /*index=5*/s32[]{:T(128)}) %tuple.56), branch_computations={%region_1.1_spmd, %region_2.3_spmd} | conditional | flops 271319040 | bytes 3694666 | solution.py:55
  50.1 0.4 multiply_reduce_fusion
  50.5 1.5 %fusion = f32[512,512]{1,0:T(8,128)S(1)} fusion(f32[512,512]{1,0:T(8,128)S(1)} %multiply_reduce_fusion, bf16[4,512,512]{2,1,0:T(8,128)(2,1)} %get-tuple-element.142, s32[]{:T(128)S(6)} %select_n.43), kind=kOutput, calls=%fused_computation.4 | convolution fusion | flops 269221888 | bytes 2621444 | tf_op jit(solution)/shard_map/while/body/eval_jaxpr/cond/branch_1_fun/dot_general | solution.py:51
  52.0 2.6 %conditional.5 = (f32[1,512,512]{2,1,0:T(8,128)S(1)}) conditional(s32[]{:T(128)} %convert_element_type.29, f32[512,512]{1,0:T(8,128)S(1)} %get-tuple-element.291, (f32[3,512]{1,0:T(4,128)S(1)}, s32[]{:T(128)}, s32[]{:T(128)}, f32[3,4,512]{2,0,1:T(4,128)S(1)}, bf16[4,512,512]{2,1,0:T(8,128)(2,1)}, /*index=5*/f32[512,512]{1,0:T(8,128)S(1)}) %tuple.63), branch_computations={%region_4.4_spmd, %region_5.6_spmd} | conditional | flops 271581184 | bytes 4743208 | solution.py:55
  52.7 0.4 multiply_reduce_fusion.1
  53.0 1.5 %fusion.6 = f32[1,512,512]{2,1,0:T(8,128)S(1)} fusion(f32[512,512]{1,0:T(8,128)S(1)} %get-tuple-element.143, f32[512,512]{1,0:T(8,128)S(1)} %multiply_reduce_fusion.1, bf16[4,512,512]{2,1,0:T(8,128)(2,1)} %get-tuple-element.148, s32[]{:T(128)S(6)} %max.8), kind=kOutput, calls=%fused_computation.13 | convolution fusion | flops 269484032 | bytes 3670020 | tf_op jit(solution)/shard_map/while/body/eval_jaxpr/cond/branch_1_fun/dot_general | solution.py:51
  54.6 1.1 constant_dynamic-update-slice_fusion.2
  55.7 0.6 dynamic_slice.61
  58.3 0.7 fusion.32
  60.3 2.5 %conditional.4 = (f32[512,512]{1,0:T(8,128)S(1)}) conditional(s32[]{:T(128)} %convert_element_type.30, () %tuple.55, (f32[3,512]{1,0:T(4,128)S(1)}, s32[]{:T(128)}, f32[3,4,512]{2,0,1:T(4,128)S(1)}, bf16[4,512,512]{2,1,0:T(8,128)(2,1)}, s32[]{:T(128)}, /*index=5*/s32[]{:T(128)}) %tuple.56), branch_computations={%region_1.1_spmd, %region_2.3_spmd} | conditional | flops 271319040 | bytes 3694666 | solution.py:55
  60.9 0.4 multiply_reduce_fusion
  61.3 1.5 %fusion = f32[512,512]{1,0:T(8,128)S(1)} fusion(f32[512,512]{1,0:T(8,128)S(1)} %multiply_reduce_fusion, bf16[4,512,512]{2,1,0:T(8,128)(2,1)} %get-tuple-element.142, s32[]{:T(128)S(6)} %select_n.43), kind=kOutput, calls=%fused_computation.4 | convolution fusion | flops 269221888 | bytes 2621444 | tf_op jit(solution)/shard_map/while/body/eval_jaxpr/cond/branch_1_fun/dot_general | solution.py:51
  62.8 2.6 %conditional.5 = (f32[1,512,512]{2,1,0:T(8,128)S(1)}) conditional(s32[]{:T(128)} %convert_element_type.29, f32[512,512]{1,0:T(8,128)S(1)} %get-tuple-element.291, (f32[3,512]{1,0:T(4,128)S(1)}, s32[]{:T(128)}, s32[]{:T(128)}, f32[3,4,512]{2,0,1:T(4,128)S(1)}, bf16[4,512,512]{2,1,0:T(8,128)(2,1)}, /*index=5*/f32[512,512]{1,0:T(8,128)S(1)}) %tuple.63), branch_computations={%region_4.4_spmd, %region_5.6_spmd} | conditional | flops 271581184 | bytes 4743208 | solution.py:55
  63.5 0.4 multiply_reduce_fusion.1
  63.8 1.5 %fusion.6 = f32[1,512,512]{2,1,0:T(8,128)S(1)} fusion(f32[512,512]{1,0:T(8,128)S(1)} %get-tuple-element.143, f32[512,512]{1,0:T(8,128)S(1)} %multiply_reduce_fusion.1, bf16[4,512,512]{2,1,0:T(8,128)(2,1)} %get-tuple-element.148, s32[]{:T(128)S(6)} %max.8), kind=kOutput, calls=%fused_computation.13 | convolution fusion | flops 269484032 | bytes 3670020 | tf_op jit(solution)/shard_map/while/body/eval_jaxpr/cond/branch_1_fun/dot_general | solution.py:51
  65.4 1.1 constant_dynamic-update-slice_fusion.2
  66.4 0.6 dynamic_slice.61
  69.1 0.7 fusion.32
  71.0 2.5 %conditional.4 = (f32[512,512]{1,0:T(8,128)S(1)}) conditional(s32[]{:T(128)} %convert_element_type.30, () %tuple.55, (f32[3,512]{1,0:T(4,128)S(1)}, s32[]{:T(128)}, f32[3,4,512]{2,0,1:T(4,128)S(1)}, bf16[4,512,512]{2,1,0:T(8,128)(2,1)}, s32[]{:T(128)}, /*index=5*/s32[]{:T(128)}) %tuple.56), branch_computations={%region_1.1_spmd, %region_2.3_spmd} | conditional | flops 271319040 | bytes 3694666 | solution.py:55
  71.6 0.4 multiply_reduce_fusion
  72.0 1.5 %fusion = f32[512,512]{1,0:T(8,128)S(1)} fusion(f32[512,512]{1,0:T(8,128)S(1)} %multiply_reduce_fusion, bf16[4,512,512]{2,1,0:T(8,128)(2,1)} %get-tuple-element.142, s32[]{:T(128)S(6)} %select_n.43), kind=kOutput, calls=%fused_computation.4 | convolution fusion | flops 269221888 | bytes 2621444 | tf_op jit(solution)/shard_map/while/body/eval_jaxpr/cond/branch_1_fun/dot_general | solution.py:51
  73.5 2.6 %conditional.5 = (f32[1,512,512]{2,1,0:T(8,128)S(1)}) conditional(s32[]{:T(128)} %convert_element_type.29, f32[512,512]{1,0:T(8,128)S(1)} %get-tuple-element.291, (f32[3,512]{1,0:T(4,128)S(1)}, s32[]{:T(128)}, s32[]{:T(128)}, f32[3,4,512]{2,0,1:T(4,128)S(1)}, bf16[4,512,512]{2,1,0:T(8,128)(2,1)}, /*index=5*/f32[512,512]{1,0:T(8,128)S(1)}) %tuple.63), branch_computations={%region_4.4_spmd, %region_5.6_spmd} | conditional | flops 271581184 | bytes 4743208 | solution.py:55
  74.6 1.5 %fusion.6 = f32[1,512,512]{2,1,0:T(8,128)S(1)} fusion(f32[512,512]{1,0:T(8,128)S(1)} %get-tuple-element.143, f32[512,512]{1,0:T(8,128)S(1)} %multiply_reduce_fusion.1, bf16[4,512,512]{2,1,0:T(8,128)(2,1)} %get-tuple-element.148, s32[]{:T(128)S(6)} %max.8), kind=kOutput, calls=%fused_computation.13 | convolution fusion | flops 269484032 | bytes 3670020 | tf_op jit(solution)/shard_map/while/body/eval_jaxpr/cond/branch_1_fun/dot_general | solution.py:51
  76.1 1.1 constant_dynamic-update-slice_fusion.2
  77.5 12.8 %collective-permute-done = f32[256,512]{0,1:T(8,128)S(1)} collective-permute-done((f32[256,512]{0,1:T(8,128)}, f32[256,512]{0,1:T(8,128)S(1)}, u32[]{:S(2)}, u32[]{:S(2)}) %collective-permute-start) | collective-permute-done | bytes 524320 | tf_op jit(solution)/shard_map/ppermute | solution.py:16
  90.3 1.1 add.83
  91.5 25.9 %collective-permute-done.1 = f32[256,512]{0,1:T(8,128)} collective-permute-done((f32[256,512]{0,1:T(8,128)S(1)}, f32[256,512]{0,1:T(8,128)}, u32[]{:S(2)}, u32[]{:S(2)}) %collective-permute-start.1) | collective-permute-done | bytes 524320 | tf_op jit(solution)/shard_map/ppermute | solution.py:16
  117.5 1.5 %convolution_convert_fusion = bf16[512,256]{1,0:T(8,128)(2,1)S(1)} fusion(bf16[256,256]{1,0:T(8,128)(2,1)S(1)} %copy-done.2, f32[256,512]{0,1:T(8,128)S(1)} %collective-permute-done, f32[256,512]{0,1:T(8,128)} %collective-permute-done.1), kind=kOutput, calls=%fused_computation.29 | convolution fusion | flops 403046400 | bytes 1441792 | tf_op jit(solution)/shard_map/dot_general | solution.py:74
  119.0 3.6 %multiply_add_fusion = f32[1024,512]{1,0:T(8,128)} fusion(f32[1024,512]{1,0:T(8,128)} %reduce-scatter.2.cloned.1.call-done, bf16[512,256]{1,0:T(8,128)(2,1)S(1)} %convolution_convert_fusion, bf16[2048,256]{1,0:T(8,128)(2,1)} %param.14, s32[]{:T(128)S(6)} %select_n.60), kind=kOutput, calls=%fused_computation.25 | convolution fusion | flops 269484032 | bytes 4980740 | tf_op jit(solution)/shard_map/dot_general | solution.py:79
  (36 shorter events, 1.4 us)
Async XLA Ops:
  7.4 1.6 %copy-start = (bf16[2048,512]{1,0:T(8,128)(2,1)S(1)}, bf16[2048,512]{1,0:T(8,128)(2,1)}, u32[]{:S(2)}) copy-start(bf16[2048,512]{1,0:T(8,128)(2,1)} %param.12) | copy-start | bytes 6291460
  7.4 69.9 %all-reduce.2.cloned.1.call-start = ((), (), s32[]{:S(2)}) async-start(), calls=%async_computation.2 | async-start | bytes 1048576 | tf_op jit(solution)/shard_map/psum | solution.py:66
  9.0 9.2 %copy-start.1 = (bf16[2048,256]{1,0:T(8,128)(2,1)S(1)}, bf16[2048,256]{1,0:T(8,128)(2,1)}, u32[]{:S(2)}) copy-start(bf16[2048,256]{1,0:T(8,128)(2,1)} %param.14) | copy-start | bytes 3145732
  18.2 3.6 %copy-start.3 = (f32[3,2048]{1,0:T(4,128)S(1)}, f32[3,2048]{1,0:T(4,128)}, u32[]{:S(2)}) copy-start(f32[3,2048]{1,0:T(4,128)} %param.13) | copy-start | bytes 73732
  21.7 97.2 %reduce-scatter.2.cloned.1.call-start = ((), (), s32[]{:S(2)}) async-start(), calls=%async_computation.1 | async-start | bytes 6291456 | tf_op jit(solution)/shard_map/reduce_scatter | solution.py:62
  31.3 2.8 %copy-start.4 = (s32[4,4]{1,0:T(4,128)S(1)}, s32[4,4]{1,0:T(4,128)}, u32[]{:S(2)}) copy-start(s32[4,4]{1,0:T(4,128)} %param.16) | copy-start | bytes 196
  77.2 40.3 %copy-start.2 = (bf16[256,256]{1,0:T(8,128)(2,1)S(1)}, bf16[256,256]{1,0:T(8,128)(2,1)}, u32[]{:S(2)}) copy-start(bf16[256,256]{1,0:T(8,128)(2,1)} %param.15) | copy-start | bytes 393220
  77.2 13.1 %collective-permute-start = (f32[256,512]{0,1:T(8,128)}, f32[256,512]{0,1:T(8,128)S(1)}, u32[]{:S(2)}, u32[]{:S(2)}) collective-permute-start(f32[256,512]{0,1:T(8,128)} %all-reduce.2.cloned.1.call-done), channel_id=1, source_target_pairs={{0,4},{4,0},{8,12},{12,8},{1,5},{5,1},{9,13},{13,9},{2,6},{6,2},{1... | collective-permute-start | bytes 1572872 | tf_op jit(solution)/shard_map/ppermute | solution.py:16
  91.4 26.0 %collective-permute-start.1 = (f32[256,512]{0,1:T(8,128)S(1)}, f32[256,512]{0,1:T(8,128)}, u32[]{:S(2)}, u32[]{:S(2)}) collective-permute-start(f32[256,512]{0,1:T(8,128)S(1)} %add.83), channel_id=1, source_target_pairs={{0,8},{4,12},{8,0},{12,4},{1,9},{5,13},{9,1},{13,5},{2,10},{6,14},... | collective-permute-start | bytes 1572872 | tf_op jit(solution)/shard_map/ppermute | solution.py:16
Sparse Core Ops, SparseCore 0:
  21.9 28.5 all-reduce.1
Sparse Core Ops, SparseCore 1:
  77.3 13.6 reduce-scatter.1
where the time goes:
time: 132 us; the launch traced here: 130 us
  waiting for transfers between devices  38.8 us (29%)
  local copies, waits for them, and re-layouts  28.4 us (22%)
  matrix products  20.6 us (16%)
  loops' own time  18.5 us (14%)
  between operations  14.9 us (11%)
  other arithmetic  8.38 us (6%)
    ppermute x2, waiting for transfers between devices, partner_2(): return lax.ppermute(value, axis, pairs)  38.8 us
    another operation x1, loops' own time, on_device(): lax.map(near_rows, jnp.arange(leaf_count, dtype=jnp.int32))  13.2 us
    dot_general x8, matrix products, add_block(): jnp.dot(kernel_block(left, right), values, preferred_element_type=jnp.flo...  12 us
    gather x1, local copies, waits for them, and re-layouts, on_device(): tree_x = jnp.take(points_x, local, axis=0)  9.2 us
    gather x2, local copies, waits for them, and re-layouts, on_device(): tree_c = jnp.take(coords, local, axis=1)  9.11 us
    another operation x8, loops' own time, leaf_sum(): total = lax.cond(ident >= 0, add_block, lambda acc: acc, total)  5.3 us
    dynamic_update_slice x4, local copies, waits for them, and re-layouts, on_device(): lax.map(near_rows, jnp.arange(leaf_count, dtype=jnp.int32))  4.27 us
    dot_general x1, matrix products, on_device(): far = jnp.dot(own_panels, mixed, preferred_element_type=jnp.float32)  3.56 us
  transfers between devices with their start and end apart: 4, of which 2 were waited for; matrix products, arithmetic and copies ran while one was open for 30% of the time, Pallas kernels for 0%

commit v1 on v0

v1 whole, which is shorter than its diff:
```python
import functools

import jax
import jax.numpy as jnp
from jax import lax
from jax.experimental import pallas as pl
from jax.experimental.pallas import tpu as pltpu
from jax.sharding import PartitionSpec as P

LEAF = 512
LANES = 128
TILE = 256
SUB = 64
FAR_AWAY = 1e18
MESH = pl.DeviceIdType.MESH

spread = 1.0 / (2.0 * 0.1 * 0.1)


def nt_dot(left, right):
    return lax.dot_general(
        left, right, (((1,), (1,)), ((), ())), preferred_element_type=jnp.float32
    )


def tn_dot(left, right):
    return lax.dot_general(
        left, right, (((0,), (0,)), ((), ())), preferred_element_type=jnp.float32
    )


def prepare_kernel(
    order_row, order_tile, coords, near_list, panels, points_x, coef_out, p_out, q_out
):
    rows = points_x.shape[0]
    nrhs = points_x.shape[1]
    rep_count = lax.axis_size("rep")
    rep = lax.axis_index("rep")
    start = (lax.axis_index("pts") * lax.axis_size("blk") + lax.axis_index("blk")) * rows
    base_leaf = start // LEAF
    half = nrhs // rep_count
    own_rows = rows // rep_count
    groups = rows // LANES
    leaf_count = rows // LEAF
    own_leaves = leaf_count // rep_count

    local = order_row[...] - start
    high = lax.shift_right_logical(local, 8)
    low = (local & (TILE - 1)).astype(jnp.float32)
    columns = pl.ds(pl.multiple_of(rep * half, LANES), half)
    lane_at = lax.broadcasted_iota(jnp.int32, (TILE, rows), 0).astype(jnp.float32).astype(jnp.bfloat16)
    total = jnp.zeros(coef_out.shape, jnp.float32)
    for tile in range(rows // TILE):
        want = jnp.where(high == tile, low, -1.0).astype(jnp.bfloat16)
        chosen = jnp.where(lane_at == want, jnp.bfloat16(1), jnp.bfloat16(0))
        moved = jnp.dot(chosen, panels[...], preferred_element_type=jnp.float32)
        total = total + tn_dot(
            points_x[pl.ds(tile * TILE, TILE), columns], moved.astype(jnp.bfloat16)
        )
    coef_out[...] = total

    per_core = own_rows // LANES
    own = order_tile[pl.ds(pl.multiple_of(rep * per_core, 8), per_core), :] - start
    own_high = lax.shift_right_logical(own, 7)
    own_low = own & (LANES - 1)
    picked = []
    for axis in range(3):
        value = jnp.zeros((per_core, LANES), jnp.float32)
        for group in range(groups):
            source = jnp.broadcast_to(
                coords[axis : axis + 1, group * LANES : (group + 1) * LANES], (per_core, LANES)
            )
            got = jnp.take_along_axis(source, own_low, axis=1, mode="promise_in_bounds")
            value = jnp.where(own_high == group, got, value)
        picked.append(value)
    blank = jnp.zeros((5, LANES), jnp.float32)
    pieces = []
    for row in range(per_core):
        pieces += [value[row : row + 1] for value in picked] + [blank]
    stacked = jnp.concatenate(pieces + [jnp.zeros((LANES - 8 * per_core, LANES), jnp.float32)], axis=0)
    turned = stacked.T
    for row in range(per_core):
        p_out[row * LANES : (row + 1) * LANES, :] = turned[:, row * 8 : (row + 1) * 8]

    high7 = lax.shift_right_logical(local, 7)
    low7 = local & (LANES - 1)
    leaf_at = lax.broadcasted_iota(jnp.int32, (1, rows), 1) // LEAF
    key = leaf_at * groups + high7
    left = (lax.broadcasted_iota(jnp.int32, (leaf_count * groups, rows), 0) == key).astype(jnp.float32)
    right = (lax.broadcasted_iota(jnp.int32, (LANES, rows), 0) == low7).astype(jnp.float32)
    member = nt_dot(left.astype(jnp.bfloat16), right.astype(jnp.bfloat16))
    folded = [
        jnp.concatenate(
            [coords[axis : axis + 1, g * LANES : (g + 1) * LANES] for g in range(groups)], axis=0
        )
        for axis in range(3)
    ]
    for own_leaf in range(own_leaves):
        leaf = rep * own_leaves + own_leaf
        live = jnp.zeros((groups, LANES), jnp.float32)
        for other in range(leaf_count):
            hit = near_list[leaf, 0] == base_leaf + other
            for slot in range(1, near_list.shape[1]):
                hit = jnp.logical_or(hit, near_list[leaf, slot] == base_leaf + other)
            weight = jnp.where(hit, 1.0, 0.0)
            live = live + weight * member[other * groups : (other + 1) * groups]
        q_out[own_leaf * groups : (own_leaf + 1) * groups, :] = jnp.where(
            live > 0.5, folded[0], FAR_AWAY
        )
    for axis in (1, 2):
        at = (own_leaves + axis - 1) * groups
        q_out[at : at + groups, :] = folded[axis]


def exchange_kernel(
    levels,
    chunks,
    coef,
    coupling,
    p_cols,
    q_rows,
    x_hbm,
    near_hbm,
    mixed_out,
    x_buf,
    k_buf,
    near_buf,
    blk_buf,
    run_buf,
    pts_buf,
    inc_buf,
    gather_buf,
    x_sem,
    near_sem,
    blk_send,
    blk_recv,
    pts_send,
    pts_recv,
    all_send,
    all_recv,
    rep_send,
    rep_recv,
):
    blk_count = lax.axis_size("blk")
    rep_count = lax.axis_size("rep")
    rep = lax.axis_index("rep")
    blk = lax.axis_index("blk")
    seg = lax.axis_index("pts")
    half = coef.shape[0]
    piece = half // blk_count
    step = piece // chunks
    groups = x_buf.shape[0] // LANES
    own_rows = p_cols.shape[0]
    own_leaves = own_rows // LEAF

    x_copy = pltpu.make_async_copy(x_hbm, x_buf, x_sem)
    x_copy.start()

    def blk_peer(d):
        return lax.rem(blk + d, blk_count)

    def rep_peer(d):
        return lax.rem(rep + d, rep_count)

    def pts_peer(bit):
        mask = 2**bit
        return seg + mask - 2 * mask * lax.rem(lax.div(seg, mask), 2)

    peers = (
        [{"blk": blk_peer(d)} for d in range(1, blk_count)]
        + [{"rep": rep_peer(d)} for d in range(1, rep_count)]
        + [{"pts": pts_peer(bit)} for bit in range(levels)]
    )
    barrier = pltpu.get_barrier_semaphore()
    for peer in peers:
        pl.semaphore_signal(barrier, inc=1, device_id=peer, device_id_type=MESH)
    pl.semaphore_wait(barrier, len(peers))

    def remote(src, dst, send, recv, peer):
        return pltpu.make_async_remote_copy(
            src_ref=src, dst_ref=dst, send_sem=send, recv_sem=recv,
            device_id=peer, device_id_type=MESH,
        )

    def rows_of(first, chunk):
        return pl.ds(pl.multiple_of(first + chunk * step, 8), step)

    blk_copies = {}
    for chunk in range(chunks):
        for d in range(1, blk_count):
            other = blk_peer(d)
            copy = remote(
                coef.at[rows_of(other * piece, chunk)],
                blk_buf.at[d - 1, pl.ds(chunk * step, step)],
                blk_send.at[d - 1, chunk],
                blk_recv.at[d - 1, chunk],
                {"blk": other},
            )
            copy.start()
            blk_copies[d, chunk] = copy

    pts_copies = {}

    def start_level(bit, chunk):
        at = pl.ds(chunk * step, step)
        copy = remote(
            run_buf.at[bit, at],
            pts_buf.at[bit, at],
            pts_send.at[bit, chunk],
            pts_recv.at[bit, chunk],
            {"pts": pts_peer(bit)},
        )
        copy.start()
        pts_copies[bit, chunk] = copy

    def reduce_blk(chunk):
        at = pl.ds(chunk * step, step)
        value = coef[rows_of(blk * piece, chunk), :]
        for d in range(1, blk_count):
            blk_copies[d, chunk].wait_recv()
            value = value + blk_buf[d - 1, at, :]
        run_buf[0, at, :] = value
        if levels:
            start_level(0, chunk)
        else:
            inc_buf[at, :] = jnp.zeros_like(value)

    all_copies = {}
    rep_copies = {}

    def level(bit, chunk):
        at = pl.ds(chunk * step, step)
        pts_copies[bit, chunk].wait_recv()
        got = pts_buf[bit, at, :]
        if bit + 1 < levels:
            run_buf[bit + 1, at, :] = run_buf[bit, at, :] + got
            start_level(bit + 1, chunk)
        scaled = 2.0 ** (-0.5 * bit) * got
        inc_buf[at, :] = scaled if bit == 0 else inc_buf[at, :] + scaled

    def mix(chunk):
        at = pl.ds(chunk * step, step)
        value = inc_buf[at, :]
        top = value.astype(jnp.bfloat16)
        rest = value - top.astype(jnp.float32)
        middle = rest.astype(jnp.bfloat16)
        bottom = (rest - middle.astype(jnp.float32)).astype(jnp.bfloat16)
        mats = coupling[...]
        mixed = nt_dot(bottom, mats) + nt_dot(middle, mats) + nt_dot(top, mats)
        own = rows_of(rep * half + blk * piece, chunk)
        gather_buf[own, :] = mixed.astype(jnp.bfloat16).astype(jnp.float32)
        for d in range(1, blk_count):
            copy = remote(
                gather_buf.at[own], gather_buf.at[own],
                all_send.at[d - 1, chunk], all_recv.at[d - 1, chunk], {"blk": blk_peer(d)},
            )
            copy.start()
            all_copies[d, chunk] = copy
        pass_on(0, chunk)

    def pass_on(back, chunk):
        if back:
            all_copies[back, chunk].wait_recv()
        source = lax.rem(blk + blk_count - back, blk_count)
        at = rows_of(rep * half + source * piece, chunk)
        for d in range(1, rep_count):
            copy = remote(
                gather_buf.at[at], gather_buf.at[at],
                rep_send.at[d - 1, back, chunk], rep_recv.at[d - 1, back, chunk],
                {"rep": rep_peer(d)},
            )
            copy.start()
            rep_copies[d, back, chunk] = copy

    near_copies = []

    def near_tile(tile):
        leaf = tile * TILE // LEAF
        for sub in range(TILE // SUB):
            at = tile * TILE + sub * SUB
            left = [
                jnp.broadcast_to(p_cols[at : at + SUB, axis : axis + 1], (SUB, LANES))
                for axis in range(3)
            ]
            for group in range(groups):
                gx = left[0] - q_rows[leaf * groups + group : leaf * groups + group + 1, :]
                rest = [
                    (own_leaves + axis - 1) * groups + group for axis in (1, 2)
                ]
                gy = left[1] - q_rows[rest[0] : rest[0] + 1, :]
                gz = left[2] - q_rows[rest[1] : rest[1] + 1, :]
                dist = gx * gx + gy * gy + gz * gz
                k_buf[sub * SUB : (sub + 1) * SUB, group * LANES : (group + 1) * LANES] = jnp.exp(
                    -dist * spread
                ).astype(jnp.bfloat16)
        near_buf[tile] = jnp.dot(
            k_buf[...], x_buf[...], preferred_element_type=jnp.float32
        ) * (LEAF ** -0.5)
        copy = pltpu.make_async_copy(
            near_buf.at[tile], near_hbm.at[pl.ds(tile * TILE, TILE)], near_sem.at[tile]
        )
        copy.start()
        near_copies.append(copy)

    work = [functools.partial(near_tile, tile) for tile in range(own_rows // TILE)]
    stages = [reduce_blk] + [functools.partial(level, bit) for bit in range(levels)] + [mix]
    x_copy.wait()
    share = max(1, len(work) // (len(stages)))
    for stage in stages[:-1]:
        for _ in range(share):
            if work:
                work.pop(0)()
        for chunk in range(chunks):
            stage(chunk)
    for chunk in range(chunks):
        mix(chunk)
    while work:
        work.pop(0)()
    for chunk in range(chunks):
        for back in range(1, blk_count):
            pass_on(back, chunk)
    for copy in rep_copies.values():
        copy.wait_recv()
    mixed_out[...] = gather_buf[...].astype(jnp.bfloat16)
    for group in (blk_copies, pts_copies, all_copies, rep_copies):
        for copy in group.values():
            copy.wait_send()
    for copy in near_copies:
        copy.wait()


def finish_kernel(mixed, near_hbm, panels_hbm, out_hbm, p_buf, buf, p_sem, in_sem, out_sem):
    tiles = buf.shape[0]
    own_rows = tiles * TILE
    rep = lax.axis_index("rep")
    p_copy = pltpu.make_async_copy(
        panels_hbm.at[pl.ds(pl.multiple_of(rep * own_rows, TILE), own_rows)], p_buf, p_sem
    )
    p_copy.start()
    loads = []
    for tile in range(tiles):
        at = pl.ds(tile * TILE, TILE)
        loads.append(pltpu.make_async_copy(near_hbm.at[at], buf.at[tile], in_sem.at[tile]))
        loads[-1].start()
    p_copy.wait()
    stores = []
    for tile in range(tiles):
        at = pl.ds(tile * TILE, TILE)
        far = nt_dot(p_buf[at, :], mixed[...])
        loads[tile].wait()
        buf[tile] = buf[tile] + far
        stores.append(pltpu.make_async_copy(buf.at[tile], out_hbm.at[at], out_sem.at[tile]))
        stores[-1].start()
    for store in stores:
        store.wait()


def on_device(points_x, coords, panels, coupling, near_list, order):
    rows, nrhs = points_x.shape
    rank = panels.shape[1]
    blk_count = lax.axis_size("blk")
    rep_count = lax.axis_size("rep")
    levels = min(lax.axis_size("pts").bit_length() - 1, 4)
    half = nrhs // rep_count
    piece = half // blk_count
    own_rows = rows // rep_count
    tiles = own_rows // TILE
    groups = rows // LANES
    own_leaves = own_rows // LEAF
    chunks = 2
    vmem = pl.BlockSpec(memory_space=pltpu.VMEM)
    smem = pl.BlockSpec(memory_space=pltpu.SMEM)
    any_space = pl.BlockSpec(memory_space=pl.ANY)
    dma = pltpu.SemaphoreType.DMA
    f32 = jnp.float32

    coef, p_cols, q_rows = pl.pallas_call(
        prepare_kernel,
        out_shape=(
            jax.ShapeDtypeStruct((half, rank), f32),
            jax.ShapeDtypeStruct((own_rows, 8), f32),
            jax.ShapeDtypeStruct(((own_leaves + 2) * groups, LANES), f32),
        ),
        in_specs=[vmem, vmem, vmem, smem, vmem, vmem],
        out_specs=(vmem, vmem, vmem),
        compiler_params=pltpu.CompilerParams(vmem_limit_bytes=48 * 2**20),
        name="prepare",
    )(order.reshape(1, rows), order.reshape(groups, LANES), coords, near_list, panels, points_x)

    near, mixed = pl.pallas_call(
        functools.partial(exchange_kernel, levels, chunks),
        out_shape=(
            jax.ShapeDtypeStruct((own_rows, nrhs), f32),
            jax.ShapeDtypeStruct((nrhs, rank), jnp.bfloat16),
        ),
        in_specs=[vmem, vmem, vmem, vmem, any_space],
        out_specs=(any_space, vmem),
        scratch_shapes=[
            pltpu.VMEM((rows, nrhs), jnp.bfloat16),
            pltpu.VMEM((TILE, rows), jnp.bfloat16),
            pltpu.VMEM((tiles, TILE, nrhs), f32),
            pltpu.VMEM((blk_count - 1, piece, rank), f32),
            pltpu.VMEM((levels, piece, rank), f32),
            pltpu.VMEM((levels, piece, rank), f32),
            pltpu.VMEM((piece, rank), f32),
            pltpu.VMEM((nrhs, rank), f32),
            dma,
            dma((tiles,)),
            dma((blk_count - 1, chunks)),
            dma((blk_count - 1, chunks)),
            dma((levels, chunks)),
            dma((levels, chunks)),
            dma((blk_count - 1, chunks)),
            dma((blk_count - 1, chunks)),
            dma((rep_count - 1, blk_count, chunks)),
            dma((rep_count - 1, blk_count, chunks)),
        ],
        compiler_params=pltpu.CompilerParams(
            collective_id=0, has_side_effects=True, vmem_limit_bytes=48 * 2**20
        ),
        name="exchange",
    )(coef, coupling, p_cols, q_rows, points_x)

    return pl.pallas_call(
        finish_kernel,
        out_shape=jax.ShapeDtypeStruct((own_rows, nrhs), f32),
        in_specs=[vmem, any_space, any_space],
        out_specs=any_space,
        scratch_shapes=[
            pltpu.VMEM((own_rows, rank), jnp.bfloat16),
            pltpu.VMEM((tiles, TILE, nrhs), f32),
            dma,
            dma((tiles,)),
            dma((tiles,)),
        ],
        compiler_params=pltpu.CompilerParams(vmem_limit_bytes=48 * 2**20),
        name="finish",
    )(mixed, near, panels)


def solution(mesh):
    placed = (
        P(("groups", "pts", "blk"), None),
        P(None, ("groups", "pts", "blk")),
        P(("groups", "pts", "blk"), None),
        P(("groups", "pts"), None),
        P(("groups", "pts", "blk"), None),
        P(("groups", "pts", "blk")),
    )
    return jax.shard_map(
        on_device,
        mesh=mesh,
        in_specs=placed,
        out_specs=P(("groups", "pts", "blk", "rep"), None),
        check_vma=False,
    )
```

time: 132 us -> 34.9 us (0.26)
  the two profiles are of different devices: /device:TPU:31 before, /device:TPU:0 now
where the time goes in v1:
time: 34.9 us; the launch traced here: 34.5 us
  Pallas kernels  29.5 us (85%)
  local copies, waits for them, and re-layouts  4.96 us (14%)
    pallas_call x1, Pallas kernels, on_device(): pl.pallas_call(functools.partial(exchange_kernel, levels, chunks), out_sh...  22.9 us
    unnamed x16, local copies, waits for them, and re-layouts  4.96 us
    pallas_call x1, Pallas kernels, on_device(): pl.pallas_call(prepare_kernel, out_shape=(jax.ShapeDtypeStruct((half, ran...  4.45 us
    pallas_call x1, Pallas kernels, on_device(): pl.pallas_call(finish_kernel, out_shape=jax.ShapeDtypeStruct((own_rows, n...  2.2 us

profile of v1, /device:TPU:0, one launch (start us, length us, event | category | flops | bytes accessed | tf_op | source)
XLA Modules:
  0.0 34.5 jit_solution(4869302593240341990)
XLA Ops:
  0.0 0.0 copy-start
  0.0 1.6 %copy-done = bf16[2048,512]{1,0:T(8,128)(2,1)S(1)} copy-done((bf16[2048,512]{1,0:T(8,128)(2,1)S(1)}, bf16[2048,512]{1,0:T(8,128)(2,1)}, u32[]{:S(2)}) %copy-start) | copy-done | bytes 2097176
  1.6 0.0 copy-start.2
  1.6 1.2 %copy-done.2 = bf16[2048,256]{1,0:T(8,128)(2,1)S(1)} copy-done((bf16[2048,256]{1,0:T(8,128)(2,1)S(1)}, bf16[2048,256]{1,0:T(8,128)(2,1)}, u32[]{:S(2)}) %copy-start.2) | copy-done | bytes 1048600
  2.8 0.0 copy-start.5
  2.8 0.8 %copy-done.5 = f32[3,2048]{1,0:T(4,128)S(1)} copy-done((f32[3,2048]{1,0:T(4,128)S(1)}, f32[3,2048]{1,0:T(4,128)}, u32[]{:S(2)}) %copy-start.5) | copy-done | bytes 24600
  3.6 0.0 copy-start.6
  3.6 0.7 %copy-done.6 = s32[2048]{0:T(1024)S(1)} copy-done((s32[2048]{0:T(1024)S(1)}, s32[2048]{0:T(1024)}, u32[]{:S(2)}) %copy-start.6) | copy-done | bytes 8216
  4.3 0.0 copy-start.7
  4.3 0.7 %copy-done.7 = s32[4,4]{1,0:T(4,128)S(1)} copy-done((s32[4,4]{1,0:T(4,128)S(1)}, s32[4,4]{1,0:T(4,128)}, u32[]{:S(2)}) %copy-start.7) | copy-done | bytes 88
  5.0 0.0 copy-start.1
  5.0 0.0 copy-start.4
  5.0 4.5 %prepare.1 = (f32[256,256]{1,0:T(8,128)S(1)}, f32[1024,8]{1,0:T(8,128)S(1)}, f32[64,128]{1,0:T(8,128)S(1)}) custom-call(s32[1,2048]{1,0:T(1,128)S(1)} %bitcast.2, s32[16,128]{1,0:T(8,128)S(1)} %bitcast.3, f32[3,2048]{1,0:T(4,128)S(1)} %copy-done.5, s32[4,4]{1,0:T(4,128)S(1)} %copy-done.7, bf16[2048,256]{1,0:T(8,128)(2,1)S(1)} %copy-done.2, ...), custom_call_target="tpu_custom_call" | custom-call | tf_op jit(solution)/shard_map/prepare/pallas_call | solution.py:377
  9.4 0.0 copy-start.3
  9.4 0.0 copy-done.1
  9.4 0.0 copy-done.4
  9.5 22.9 %exchange.1 = (f32[1024,512]{1,0:T(8,128)S(1)}, bf16[512,256]{1,0:T(8,128)(2,1)S(1)}) custom-call(f32[256,256]{1,0:T(8,128)S(1)} %get-tuple-element.10.coef, bf16[256,256]{1,0:T(8,128)(2,1)S(1)} %copy-done.4, f32[1024,8]{1,0:T(8,128)S(1)} %get-tuple-element.11.p_cols, f32[64,128]{1,0:T(8,128)S(1)} %get-tuple-element.12.q_rows, bf16[2048,512]{1,0:T(8,128)(2,1)S(1)} %copy-done.1), custom_call_target="tpu_custom_call" | custom-call | tf_op jit(solution)/shard_map/exchange/pallas_call | solution.py:390
  32.3 0.0 copy-done.3
  32.3 2.2 %finish.1 = f32[1024,512]{1,0:T(8,128)} custom-call(bf16[512,256]{1,0:T(8,128)(2,1)S(1)} %get-tuple-element.13.mixed, f32[1024,512]{1,0:T(8,128)S(1)} %get-tuple-element.14.near_hbm, bf16[2048,256]{1,0:T(8,128)(2,1)S(1)} %copy-done.3), custom_call_target="tpu_custom_call" | custom-call | tf_op jit(solution)/shard_map/finish/pallas_call | solution.py:424
Async XLA Ops:
  0.0 1.6 %copy-start = (bf16[2048,512]{1,0:T(8,128)(2,1)S(1)}, bf16[2048,512]{1,0:T(8,128)(2,1)}, u32[]{:S(2)}) copy-start(bf16[2048,512]{1,0:T(8,128)(2,1)} %x_hbm.1) | copy-start | bytes 6291460
  1.6 1.2 %copy-start.2 = (bf16[2048,256]{1,0:T(8,128)(2,1)S(1)}, bf16[2048,256]{1,0:T(8,128)(2,1)}, u32[]{:S(2)}) copy-start(bf16[2048,256]{1,0:T(8,128)(2,1)} %panels_hbm.1) | copy-start | bytes 3145732
  2.8 0.8 %copy-start.5 = (f32[3,2048]{1,0:T(4,128)S(1)}, f32[3,2048]{1,0:T(4,128)}, u32[]{:S(2)}) copy-start(f32[3,2048]{1,0:T(4,128)} %coords.1) | copy-start | bytes 73732
  3.6 0.7 %copy-start.6 = (s32[2048]{0:T(1024)S(1)}, s32[2048]{0:T(1024)}, u32[]{:S(2)}) copy-start(s32[2048]{0:T(1024)} %param.11) | copy-start | bytes 24580
  4.3 0.7 %copy-start.7 = (s32[4,4]{1,0:T(4,128)S(1)}, s32[4,4]{1,0:T(4,128)}, u32[]{:S(2)}) copy-start(s32[4,4]{1,0:T(4,128)} %near_list.1) | copy-start | bytes 196
  5.0 4.5 %copy-start.1 = (bf16[2048,512]{1,0:T(8,128)(2,1)S(1)}, bf16[2048,512]{1,0:T(8,128)(2,1)}, u32[]{:S(2)}) copy-start(bf16[2048,512]{1,0:T(8,128)(2,1)} %x_hbm.1) | copy-start | bytes 6291460
  5.0 4.5 %copy-start.4 = (bf16[256,256]{1,0:T(8,128)(2,1)S(1)}, bf16[256,256]{1,0:T(8,128)(2,1)}, u32[]{:S(2)}) copy-start(bf16[256,256]{1,0:T(8,128)(2,1)} %coupling.1) | copy-start | bytes 393220
  9.4 22.9 %copy-start.3 = (bf16[2048,256]{1,0:T(8,128)(2,1)S(1)}, bf16[2048,256]{1,0:T(8,128)(2,1)}, u32[]{:S(2)}) copy-start(bf16[2048,256]{1,0:T(8,128)(2,1)} %panels_hbm.1) | copy-start | bytes 3145732

commit v2 on v0

v2 whole, which is shorter than its diff:
```python
import functools

import jax
import jax.numpy as jnp
from jax import lax
from jax.experimental import pallas as pl
from jax.experimental.pallas import tpu as pltpu
from jax.sharding import PartitionSpec as P

LEAF = 512
LANES = 128
TILE = 256
SUB = 64
FAR_AWAY = 1e18
CHUNKS = 2
NEAR_WAVES = (0, 0, 2, 4)
VMEM_MIB = 44
MESH = pl.DeviceIdType.MESH

spread = 1.0 / (2.0 * 0.1 * 0.1)


def nt_dot(left, right):
    return lax.dot_general(
        left, right, (((1,), (1,)), ((), ())), preferred_element_type=jnp.float32
    )


def tn_dot(left, right):
    return lax.dot_general(
        left, right, (((0,), (0,)), ((), ())), preferred_element_type=jnp.float32
    )


def exchange_kernel(
    levels,
    chunks,
    near_waves,
    order_row_hbm,
    order_tile_hbm,
    coords_hbm,
    list_hbm,
    panels_hbm,
    coupling_hbm,
    x_hbm,
    near_out,
    mixed_out,
    order_row,
    order_tile,
    coords,
    near_list,
    panels,
    coupling,
    x_buf,
    p_cols,
    q_rows,
    coef,
    k_buf,
    near_buf,
    part_buf,
    run_buf,
    pts_buf,
    inc_buf,
    all_buf,
    gather_buf,
    load_sem,
    near_sem,
    part_send,
    part_recv,
    pts_send,
    pts_recv,
    all_send,
    all_recv,
    rep_send,
    rep_recv,
):
    blk_count = lax.axis_size("blk")
    rep_count = lax.axis_size("rep")
    rep = lax.axis_index("rep")
    blk = lax.axis_index("blk")
    seg = lax.axis_index("pts")
    rows, nrhs = x_buf.shape
    start = (seg * blk_count + blk) * rows
    base_leaf = start // LEAF
    half = nrhs // rep_count
    piece = half // (2 * blk_count)
    step = piece // chunks
    groups = rows // LANES
    own_rows = rows // rep_count
    leaf_count = rows // LEAF
    own_leaves = own_rows // LEAF

    loads = []
    for source, target in (
        (order_row_hbm, order_row),
        (panels_hbm, panels),
        (x_hbm, x_buf),
        (order_tile_hbm, order_tile),
        (coords_hbm, coords),
        (list_hbm, near_list),
        (coupling_hbm, coupling),
    ):
        loads.append(pltpu.make_async_copy(source, target, load_sem.at[len(loads)]))
        loads[-1].start()

    def blk_peer(d):
        return lax.rem(blk + d, blk_count)

    def rep_peer(d):
        return lax.rem(rep + d, rep_count)

    def pts_peer(bit):
        mask = 2**bit
        return seg + mask - 2 * mask * lax.rem(lax.div(seg, mask), 2)

    offsets = [(other, d) for other in range(2) for d in range(blk_count)]

    def block_peer(other, d):
        return {"pts": pts_peer(0) if other else seg, "blk": blk_peer(d)}

    def slice_of(other, d):
        side = lax.rem(seg, 2)
        return ((1 - side if other else side) * blk_count + blk_peer(d)) * piece

    peers = [block_peer(*offset) for offset in offsets[1:]]
    peers += [{"rep": rep_peer(d)} for d in range(1, rep_count)]
    peers += [{"pts": pts_peer(bit)} for bit in range(1, levels)]
    barrier = pltpu.get_barrier_semaphore()
    for peer in peers:
        pl.semaphore_signal(barrier, inc=1, device_id=peer, device_id_type=MESH)

    loads[0].wait()
    local = order_row[...] - start
    high = lax.shift_right_logical(local, 8)
    low = (local & (TILE - 1)).astype(jnp.float32)
    columns = pl.ds(pl.multiple_of(rep * half, LANES), half)
    lane_at = (
        lax.broadcasted_iota(jnp.int32, (TILE, rows), 0).astype(jnp.float32).astype(jnp.bfloat16)
    )
    total = jnp.zeros(coef.shape, jnp.float32)
    for tile in range(rows // TILE):
        want = jnp.where(high == tile, low, -1.0).astype(jnp.bfloat16)
        chosen = jnp.where(lane_at == want, jnp.bfloat16(1), jnp.bfloat16(0))
        if tile == 0:
            loads[1].wait()
        moved = jnp.dot(chosen, panels[...], preferred_element_type=jnp.float32)
        if tile == 0:
            loads[2].wait()
        total = total + tn_dot(
            x_buf[pl.ds(tile * TILE, TILE), columns], moved.astype(jnp.bfloat16)
        )
    coef[...] = total

    pl.semaphore_wait(barrier, len(peers))

    def remote(src, dst, send, recv, peer):
        return pltpu.make_async_remote_copy(
            src_ref=src, dst_ref=dst, send_sem=send, recv_sem=recv,
            device_id=peer, device_id_type=MESH,
        )

    def rows_of(first, chunk):
        return pl.ds(pl.multiple_of(first + chunk * step, 8), step)

    def at_of(chunk):
        return pl.ds(chunk * step, step)

    def part_copy(at, chunk):
        return remote(
            coef.at[rows_of(slice_of(*offsets[at]), chunk)],
            part_buf.at[at, at_of(chunk)],
            part_send.at[at, chunk],
            part_recv.at[at, chunk],
            block_peer(*offsets[at]),
        )

    def level_copy(bit, chunk):
        return remote(
            run_buf.at[bit - 1, at_of(chunk)],
            pts_buf.at[bit - 1, at_of(chunk)],
            pts_send.at[bit - 1, chunk],
            pts_recv.at[bit - 1, chunk],
            {"pts": pts_peer(bit)},
        )

    def all_copy(at, chunk):
        return remote(
            inc_buf.at[offsets[at][0], at_of(chunk)],
            all_buf.at[at, at_of(chunk)],
            all_send.at[at, chunk],
            all_recv.at[at, chunk],
            block_peer(*offsets[at]),
        )

    def source_rows(at, chunk):
        other, d = offsets[at]
        return rows_of(rep * half + slice_of(other, blk_count - d), chunk)

    def rep_copy(d, at, chunk):
        rows_at = source_rows(at, chunk)
        return remote(
            gather_buf.at[rows_at], gather_buf.at[rows_at],
            rep_send.at[d - 1, at, chunk], rep_recv.at[d - 1, at, chunk],
            {"rep": rep_peer(d)},
        )

    for chunk in range(chunks):
        for at in range(1, len(offsets)):
            part_copy(at, chunk).start()

    def reduce_parts(chunk):
        at = at_of(chunk)
        sums = [coef[rows_of(slice_of(0, 0), chunk), :], None]
        for index in range(1, len(offsets)):
            part_copy(index, chunk).wait_recv()
            got = part_buf[index, at, :]
            other = offsets[index][0]
            sums[other] = got if sums[other] is None else sums[other] + got
        run_buf[0, at, :] = sums[0] + sums[1]
        if levels > 1:
            level_copy(1, chunk).start()
        inc_buf[0, at, :] = sums[1]
        inc_buf[1, at, :] = sums[0]
        if levels == 1:
            share(chunk)

    def level(bit, chunk):
        at = at_of(chunk)
        level_copy(bit, chunk).wait_recv()
        got = pts_buf[bit - 1, at, :]
        if bit + 1 < levels:
            run_buf[bit, at, :] = run_buf[bit - 1, at, :] + got
            level_copy(bit + 1, chunk).start()
        scaled = 2.0 ** (-0.5 * bit) * got
        for other in range(2):
            inc_buf[other, at, :] = inc_buf[other, at, :] + scaled
        if bit + 1 == levels:
            share(chunk)

    def mix(at, chunk, value):
        top = value.astype(jnp.bfloat16)
        rest = value - top.astype(jnp.float32)
        middle = rest.astype(jnp.bfloat16)
        bottom = (rest - middle.astype(jnp.float32)).astype(jnp.bfloat16)
        mats = coupling[...]
        mixed = nt_dot(bottom, mats) + nt_dot(middle, mats) + nt_dot(top, mats)
        gather_buf[source_rows(at, chunk), :] = mixed.astype(jnp.bfloat16).astype(jnp.float32)
        for d in range(1, rep_count):
            rep_copy(d, at, chunk).start()

    def share(chunk):
        for index in range(1, len(offsets)):
            all_copy(index, chunk).start()
        mix(0, chunk, inc_buf[0, at_of(chunk), :])

    def pass_on(chunk):
        for index in range(1, len(offsets)):
            all_copy(index, chunk).wait_recv()
            mix(index, chunk, all_buf[index, at_of(chunk), :])

    for load in loads[3:]:
        load.wait()
    per_core = own_rows // LANES
    own = order_tile[pl.ds(pl.multiple_of(rep * per_core, 8), per_core), :] - start
    own_high = lax.shift_right_logical(own, 7)
    own_low = own & (LANES - 1)
    picked = []
    for axis in range(3):
        value = jnp.zeros((per_core, LANES), jnp.float32)
        for group in range(groups):
            source = jnp.broadcast_to(
                coords[axis : axis + 1, group * LANES : (group + 1) * LANES], (per_core, LANES)
            )
            got = jnp.take_along_axis(source, own_low, axis=1, mode="promise_in_bounds")
            value = jnp.where(own_high == group, got, value)
        picked.append(value)
    blank = jnp.zeros((5, LANES), jnp.float32)
    pieces = []
    for row in range(per_core):
        pieces += [value[row : row + 1] for value in picked] + [blank]
    pieces.append(jnp.zeros((LANES - 8 * per_core, LANES), jnp.float32))
    turned = jnp.concatenate(pieces, axis=0).T
    for row in range(per_core):
        p_cols[row * LANES : (row + 1) * LANES, :] = turned[:, row * 8 : (row + 1) * 8]

    high7 = lax.shift_right_logical(local, 7)
    low7 = local & (LANES - 1)
    leaf_at = lax.broadcasted_iota(jnp.int32, (1, rows), 1) // LEAF
    key = leaf_at * groups + high7
    left = lax.broadcasted_iota(jnp.int32, (leaf_count * groups, rows), 0) == key
    right = lax.broadcasted_iota(jnp.int32, (LANES, rows), 0) == low7
    member = nt_dot(
        jnp.where(left, 1.0, 0.0).astype(jnp.bfloat16),
        jnp.where(right, 1.0, 0.0).astype(jnp.bfloat16),
    )
    folded = [
        jnp.concatenate(
            [coords[axis : axis + 1, g * LANES : (g + 1) * LANES] for g in range(groups)], axis=0
        )
        for axis in range(3)
    ]
    for own_leaf in range(own_leaves):
        entries = near_list[pl.ds(rep * own_leaves + own_leaf, 1), :] - base_leaf
        live = jnp.zeros((groups, LANES), jnp.float32)
        for other in range(leaf_count):
            hit = jnp.where(entries == other, 1.0, 0.0)
            weight = jnp.sum(hit, axis=1, keepdims=True)
            live = live + weight * member[other * groups : (other + 1) * groups]
        q_rows[own_leaf * groups : (own_leaf + 1) * groups, :] = jnp.where(
            live > 0.5, folded[0], FAR_AWAY
        )
    for axis in (1, 2):
        at = (own_leaves + axis - 1) * groups
        q_rows[at : at + groups, :] = folded[axis]

    def near_tile(tile):
        leaf = tile * TILE // LEAF
        for sub in range(TILE // SUB):
            at = tile * TILE + sub * SUB
            left = [
                jnp.broadcast_to(p_cols[at : at + SUB, axis : axis + 1], (SUB, LANES))
                for axis in range(3)
            ]
            for group in range(groups):
                gap = []
                for axis in range(3):
                    row = (leaf if axis == 0 else own_leaves + axis - 1) * groups + group
                    gap.append(left[axis] - q_rows[row : row + 1, :])
                dist = gap[0] * gap[0] + gap[1] * gap[1] + gap[2] * gap[2]
                k_buf[sub * SUB : (sub + 1) * SUB, group * LANES : (group + 1) * LANES] = jnp.exp(
                    -dist * spread
                ).astype(jnp.bfloat16)
        near_buf[tile] = jnp.dot(
            k_buf[...], x_buf[...], preferred_element_type=jnp.float32
        ) * (LEAF ** -0.5)
        near_copy(tile).start()

    def near_copy(tile):
        return pltpu.make_async_copy(
            near_buf.at[tile], near_out.at[pl.ds(tile * TILE, TILE)], near_sem.at[tile]
        )

    stages = [reduce_parts]
    stages += [functools.partial(level, bit) for bit in range(1, levels)]
    stages.append(pass_on)
    lag = chunks
    tile_at = 0
    for wave in range(chunks + lag * (len(stages) - 1)):
        for _ in range(near_waves.count(wave)):
            if tile_at < own_rows // TILE:
                near_tile(tile_at)
                tile_at += 1
        for at, stage in enumerate(stages):
            chunk = wave - lag * at
            if 0 <= chunk < chunks:
                stage(chunk)
    for tile in range(tile_at, own_rows // TILE):
        near_tile(tile)
    for chunk in range(chunks):
        for at in range(len(offsets)):
            for d in range(1, rep_count):
                rep_copy(d, at, chunk).wait_recv()
    mixed_out[...] = gather_buf[...].astype(jnp.bfloat16)
    for chunk in range(chunks):
        for at in range(len(offsets)):
            if at:
                part_copy(at, chunk).wait_send()
                all_copy(at, chunk).wait_send()
            for d in range(1, rep_count):
                rep_copy(d, at, chunk).wait_send()
        for bit in range(1, levels):
            level_copy(bit, chunk).wait_send()
    for tile in range(own_rows // TILE):
        near_copy(tile).wait()


def finish_kernel(mixed, near, panels, out_hbm, buf, out_sem):
    tiles = buf.shape[0]
    rep = lax.axis_index("rep")
    stores = []
    for tile in range(tiles):
        at = pl.ds(tile * TILE, TILE)
        own = pl.ds(pl.multiple_of((rep * tiles + tile) * TILE, TILE), TILE)
        buf[tile] = near[at, :] + nt_dot(panels[own, :], mixed[...])
        stores.append(pltpu.make_async_copy(buf.at[tile], out_hbm.at[at], out_sem.at[tile]))
        stores[-1].start()
    for store in stores:
        store.wait()


def on_device(points_x, coords, panels, coupling, near_list, order):
    rows, nrhs = points_x.shape
    rank = panels.shape[1]
    blk_count = lax.axis_size("blk")
    rep_count = lax.axis_size("rep")
    levels = min(lax.axis_size("pts").bit_length() - 1, 4)
    half = nrhs // rep_count
    piece = half // (2 * blk_count)
    own_rows = rows // rep_count
    tiles = own_rows // TILE
    groups = rows // LANES
    own_leaves = own_rows // LEAF
    chunks = CHUNKS
    slots = max(levels - 1, 1)
    members = 2 * blk_count
    vmem = pl.BlockSpec(memory_space=pltpu.VMEM)
    any_space = pl.BlockSpec(memory_space=pl.ANY)
    dma = pltpu.SemaphoreType.DMA
    f32 = jnp.float32
    bf16 = jnp.bfloat16

    operands = (
        order.reshape(1, rows), order.reshape(groups, LANES), coords, near_list, panels, coupling, points_x
    )
    near, mixed = pl.pallas_call(
        functools.partial(exchange_kernel, levels, chunks, NEAR_WAVES),
        out_shape=(
            jax.ShapeDtypeStruct((own_rows, nrhs), f32),
            jax.ShapeDtypeStruct((nrhs, rank), bf16),
        ),
        in_specs=[pl.BlockSpec(memory_space=pltpu.HBM)] * 7,
        out_specs=(any_space, vmem),
        scratch_shapes=[
            pltpu.VMEM((1, rows), jnp.int32),
            pltpu.VMEM((groups, LANES), jnp.int32),
            pltpu.VMEM((3, rows), f32),
            pltpu.VMEM(near_list.shape, jnp.int32),
            pltpu.VMEM((rows, rank), bf16),
            pltpu.VMEM((rank, rank), bf16),
            pltpu.VMEM((rows, nrhs), bf16),
            pltpu.VMEM((own_rows, 8), f32),
            pltpu.VMEM(((own_leaves + 2) * groups, LANES), f32),
            pltpu.VMEM((half, rank), f32),
            pltpu.VMEM((TILE, rows), bf16),
            pltpu.VMEM((tiles, TILE, nrhs), f32),
            pltpu.VMEM((members, piece, rank), f32),
            pltpu.VMEM((slots, piece, rank), f32),
            pltpu.VMEM((slots, piece, rank), f32),
            pltpu.VMEM((2, piece, rank), f32),
            pltpu.VMEM((members, piece, rank), f32),
            pltpu.VMEM((nrhs, rank), f32),
            dma((7,)),
            dma((tiles,)),
            dma((members, chunks)),
            dma((members, chunks)),
            dma((slots, chunks)),
            dma((slots, chunks)),
            dma((members, chunks)),
            dma((members, chunks)),
            dma((rep_count - 1, members, chunks)),
            dma((rep_count - 1, members, chunks)),
        ],
        compiler_params=pltpu.CompilerParams(
            collective_id=0, has_side_effects=True, vmem_limit_bytes=VMEM_MIB * 2**20
        ),
        name="exchange",
    )(*[pltpu.with_memory_space_constraint(value, pltpu.HBM) for value in operands])

    return pl.pallas_call(
        finish_kernel,
        out_shape=jax.ShapeDtypeStruct((own_rows, nrhs), f32),
        in_specs=[vmem, vmem, vmem],
        out_specs=any_space,
        scratch_shapes=[
            pltpu.VMEM((tiles, TILE, nrhs), f32),
            dma((tiles,)),
        ],
        compiler_params=pltpu.CompilerParams(vmem_limit_bytes=32 * 2**20),
        name="finish",
    )(mixed, near, panels)


def solution(mesh):
    placed = (
        P(("groups", "pts", "blk"), None),
        P(None, ("groups", "pts", "blk")),
        P(("groups", "pts", "blk"), None),
        P(("groups", "pts"), None),
        P(("groups", "pts", "blk"), None),
        P(("groups", "pts", "blk")),
    )
    return jax.shard_map(
        on_device,
        mesh=mesh,
        in_specs=placed,
        out_specs=P(("groups", "pts", "blk", "rep"), None),
        check_vma=False,
    )
```

time: 132 us -> 25.7 us (0.19)
  the two profiles are of different devices: /device:TPU:31 before, /device:TPU:0 now
where the time goes in v2:
time: 25.7 us; the launch traced here: 25.6 us
  Pallas kernels  25.6 us (100%)
    pallas_call x1, Pallas kernels, on_device(): pl.pallas_call(functools.partial(exchange_kernel, levels, chunks, NEAR_WA...  23.9 us
    pallas_call x1, Pallas kernels, on_device(): pl.pallas_call(finish_kernel, out_shape=jax.ShapeDtypeStruct((own_rows, n...  1.61 us

profile of v2, /device:TPU:0, one launch (start us, length us, event | category | flops | bytes accessed | tf_op | source)
XLA Modules:
  0.0 25.6 jit_solution(2924653907029083004)
XLA Ops:
  0.0 0.0 copy-start
  0.0 23.9 %exchange.1 = (f32[1024,512]{1,0:T(8,128)S(1)}, bf16[512,256]{1,0:T(8,128)(2,1)S(1)}) custom-call(s32[1,2048]{1,0:T(1,128)} %bitcast.2, s32[16,128]{1,0:T(8,128)} %bitcast.3, f32[3,2048]{1,0:T(4,128)} %coords_hbm.1, s32[4,4]{1,0:T(4,128)} %list_hbm.1, bf16[2048,256]{1,0:T(8,128)(2,1)} %panels.1, bf16[256,256]{1,0:T(8,128)(2,1)} %coupling_hbm.1, ...), custom_call_target="tpu_custom_call" | custom-call | tf_op jit(solution)/shard_map/exchange/pallas_call | solution.py:415
  24.0 0.0 copy-done
  24.0 1.6 %finish.1 = f32[1024,512]{1,0:T(8,128)} custom-call(bf16[512,256]{1,0:T(8,128)(2,1)S(1)} %get-tuple-element.7.mixed, f32[1024,512]{1,0:T(8,128)S(1)} %get-tuple-element.8.near, bf16[2048,256]{1,0:T(8,128)(2,1)S(1)} %copy-done), custom_call_target="tpu_custom_call" | custom-call | tf_op jit(solution)/shard_map/finish/pallas_call | solution.py:459
Async XLA Ops:
  0.0 24.0 %copy-start = (bf16[2048,256]{1,0:T(8,128)(2,1)S(1)}, bf16[2048,256]{1,0:T(8,128)(2,1)}, u32[]{:S(2)}) copy-start(bf16[2048,256]{1,0:T(8,128)(2,1)} %panels.1) | copy-start | bytes 3145732

commit v3 on v2

--- a/solution.py
+++ b/solution.py
@@ -137,18 +137,17 @@
     lane_at = (
         lax.broadcasted_iota(jnp.int32, (TILE, rows), 0).astype(jnp.float32).astype(jnp.bfloat16)
     )
-    total = jnp.zeros(coef.shape, jnp.float32)
+    lows = jnp.where(lane_at == low.astype(jnp.bfloat16), jnp.bfloat16(1), jnp.bfloat16(0))
+    moved = []
     for tile in range(rows // TILE):
-        want = jnp.where(high == tile, low, -1.0).astype(jnp.bfloat16)
-        chosen = jnp.where(lane_at == want, jnp.bfloat16(1), jnp.bfloat16(0))
+        chosen = lows * jnp.where(high == tile, 1.0, 0.0).astype(jnp.bfloat16)
         if tile == 0:
             loads[1].wait()
-        moved = jnp.dot(chosen, panels[...], preferred_element_type=jnp.float32)
-        if tile == 0:
-            loads[2].wait()
-        total = total + tn_dot(
-            x_buf[pl.ds(tile * TILE, TILE), columns], moved.astype(jnp.bfloat16)
-        )
+        moved.append(
+            jnp.dot(chosen, panels[...], preferred_element_type=jnp.float32).astype(jnp.bfloat16)
+        )
+    loads[2].wait()
+    total = tn_dot(x_buf[:, columns], jnp.concatenate(moved, axis=0))
     coef[...] = total
 
     pl.semaphore_wait(barrier, len(peers))

time: 25.7 us -> 24.4 us (0.949)
  Pallas kernels: 25.6 us -> 24.2 us
    pallas_call x1, Pallas kernels: 23.9 us -> 22.6 us  [on_device(): pl.pallas_call(functools.partial(exchange_kernel, levels, chunks, NEAR_WA...]
where the time goes in v3:
time: 24.4 us; the launch traced here: 24.2 us
  Pallas kernels  24.2 us (99%)
    pallas_call x1, Pallas kernels, on_device(): pl.pallas_call(functools.partial(exchange_kernel, levels, chunks, NEAR_WA...  22.6 us
    pallas_call x1, Pallas kernels, on_device(): pl.pallas_call(finish_kernel, out_shape=jax.ShapeDtypeStruct((own_rows, n...  1.61 us

profile of v3, /device:TPU:0, one launch (start us, length us, event | category | flops | bytes accessed | tf_op | source)
XLA Modules:
  0.0 24.2 jit_solution(17724216509255845966)
XLA Ops:
  0.0 0.0 copy-start
  0.0 22.6 %exchange.1 = (f32[1024,512]{1,0:T(8,128)S(1)}, bf16[512,256]{1,0:T(8,128)(2,1)S(1)}) custom-call(s32[1,2048]{1,0:T(1,128)} %bitcast.2, s32[16,128]{1,0:T(8,128)} %bitcast.3, f32[3,2048]{1,0:T(4,128)} %coords_hbm.1, s32[4,4]{1,0:T(4,128)} %list_hbm.1, bf16[2048,256]{1,0:T(8,128)(2,1)} %panels.1, bf16[256,256]{1,0:T(8,128)(2,1)} %coupling_hbm.1, ...), custom_call_target="tpu_custom_call" | custom-call | tf_op jit(solution)/shard_map/exchange/pallas_call | solution.py:414
  22.6 0.0 copy-done
  22.6 1.6 %finish.1 = f32[1024,512]{1,0:T(8,128)} custom-call(bf16[512,256]{1,0:T(8,128)(2,1)S(1)} %get-tuple-element.7.mixed, f32[1024,512]{1,0:T(8,128)S(1)} %get-tuple-element.8.near, bf16[2048,256]{1,0:T(8,128)(2,1)S(1)} %copy-done), custom_call_target="tpu_custom_call" | custom-call | tf_op jit(solution)/shard_map/finish/pallas_call | solution.py:458
Async XLA Ops:
  0.0 22.6 %copy-start = (bf16[2048,256]{1,0:T(8,128)(2,1)S(1)}, bf16[2048,256]{1,0:T(8,128)(2,1)}, u32[]{:S(2)}) copy-start(bf16[2048,256]{1,0:T(8,128)(2,1)} %panels.1) | copy-start | bytes 3145732

commit v4 on v3

--- a/solution.py
+++ b/solution.py
@@ -13,7 +13,7 @@
 SUB = 64
 FAR_AWAY = 1e18
 CHUNKS = 2
-NEAR_WAVES = (0, 0, 2, 4)
+NEAR_WAVES = (0, 2, 2, 4)
 VMEM_MIB = 44
 MESH = pl.DeviceIdType.MESH
 

time: 24.4 us -> 24.3 us (level)
  no operation moved by 1% of the time
where the time goes in v4:
time: 24.3 us; the launch traced here: 24.1 us
  Pallas kernels  24.1 us (99%)
    pallas_call x1, Pallas kernels, on_device(): pl.pallas_call(functools.partial(exchange_kernel, levels, chunks, NEAR_WA...  22.5 us
    pallas_call x1, Pallas kernels, on_device(): pl.pallas_call(finish_kernel, out_shape=jax.ShapeDtypeStruct((own_rows, n...  1.61 us

profile of v4, /device:TPU:0, one launch (start us, length us, event | category | flops | bytes accessed | tf_op | source)
XLA Modules:
  0.0 24.1 jit_solution(4629884408332778556)
XLA Ops:
  0.0 0.0 copy-start
  0.0 22.5 %exchange.1 = (f32[1024,512]{1,0:T(8,128)S(1)}, bf16[512,256]{1,0:T(8,128)(2,1)S(1)}) custom-call(s32[1,2048]{1,0:T(1,128)} %bitcast.2, s32[16,128]{1,0:T(8,128)} %bitcast.3, f32[3,2048]{1,0:T(4,128)} %coords_hbm.1, s32[4,4]{1,0:T(4,128)} %list_hbm.1, bf16[2048,256]{1,0:T(8,128)(2,1)} %panels.1, bf16[256,256]{1,0:T(8,128)(2,1)} %coupling_hbm.1, ...), custom_call_target="tpu_custom_call" | custom-call | tf_op jit(solution)/shard_map/exchange/pallas_call | solution.py:414
  22.5 0.0 copy-done
  22.5 1.6 %finish.1 = f32[1024,512]{1,0:T(8,128)} custom-call(bf16[512,256]{1,0:T(8,128)(2,1)S(1)} %get-tuple-element.7.mixed, f32[1024,512]{1,0:T(8,128)S(1)} %get-tuple-element.8.near, bf16[2048,256]{1,0:T(8,128)(2,1)S(1)} %copy-done), custom_call_target="tpu_custom_call" | custom-call | tf_op jit(solution)/shard_map/finish/pallas_call | solution.py:458
Async XLA Ops:
  0.0 22.5 %copy-start = (bf16[2048,256]{1,0:T(8,128)(2,1)S(1)}, bf16[2048,256]{1,0:T(8,128)(2,1)}, u32[]{:S(2)}) copy-start(bf16[2048,256]{1,0:T(8,128)(2,1)} %panels.1) | copy-start | bytes 3145732
